TPU v7x, 256 devices: a whole 4x4x8 slice. The times are simulated.
256 devices in a mesh: pair: 4 (over y_lo, core), row: 64 (over y_hi, x, z).
Axes of the slice: x: 4, y: 4 (y_hi: 2, y_lo: 2; y = y_hi * 2 + y_lo), z: 8, core: 2. Of those that a mesh axis runs over, the one named last changes fastest.
Arguments:
- integrals: float32 [128, 1600, 1600], P('pair', 'row'), may hold values from -6 to 6
- coeffs: float32 [1600, 1024], replicated, may hold values from -0.15625 to 0.15625
- pair_list: int32 [128, 2], replicated, may hold values from 0 to 1599, as said below
Outputs:
- transformed: float32 [1024, 64, 1024], P(('pair', 'row'))
Inputs may be any that keep to these rules, and one draw needn't show every extreme that they name: `pair_list`: each row is a pair (p, q) of atomic orbital indices with p >= q; some rows have p == q.
All inputs are finite; a program needn't handle non-finite values.
Results may differ from a plain program's by a relative error of at most 0.000071.
Values sent between devices are 32-bit elements; how exact they have to be, the bound alone decides.
A program may use at most 128 MiB of HBM per device.

v0:
```python
import jax
import jax.numpy as jnp
from jax import lax
from jax.sharding import PartitionSpec as P

NACT = 8


def pair_weights(coeffs, pair_list, active):
    high = lax.Precision.HIGHEST
    basis = coeffs.shape[0]
    block = coeffs[:, :active]
    columns = lax.broadcasted_iota(jnp.int32, (pair_list.shape[0], basis), 1)
    pick_first = (columns == pair_list[:, 0:1]).astype(jnp.float32)
    pick_second = (columns == pair_list[:, 1:2]).astype(jnp.float32)
    first = jnp.dot(pick_first, block, precision=high, preferred_element_type=jnp.float32)
    second = jnp.dot(pick_second, block, precision=high, preferred_element_type=jnp.float32)
    distinct = (pair_list[:, 0] != pair_list[:, 1]).astype(jnp.float32)
    weights = jnp.einsum("ni,nj->ijn", first, second) + distinct[None, None, :] * jnp.einsum(
        "ni,nj->ijn", second, first
    )
    return weights.reshape(active * active, pair_list.shape[0])


def body(integrals, coeffs, pair_list):
    high = lax.Precision.HIGHEST
    pair_dev, rows_dev, basis = integrals.shape
    orbitals = coeffs.shape[1]
    pair_count = lax.axis_size("pair")
    row_count = lax.axis_size("row")
    local_b = orbitals // (pair_count * row_count)
    flat = integrals.reshape(pair_dev * rows_dev, basis)
    weights = pair_weights(coeffs, pair_list, NACT)
    factor = basis / jnp.sqrt(jnp.float32(2 * pair_list.shape[0]))
    quarter_s = lax.dot_general(
        coeffs, flat, (((0,), (1,)), ((), ())), precision=high, preferred_element_type=jnp.float32
    )
    packed = quarter_s.reshape(pair_count, 1, row_count, 1, local_b * pair_dev * rows_dev)
    moved = lax.all_to_all(
        lax.all_to_all(packed, "pair", split_axis=0, concat_axis=1, tiled=True),
        "row",
        split_axis=2,
        concat_axis=3,
        tiled=True,
    )
    moved = moved.reshape(pair_count, row_count, local_b, pair_dev, rows_dev)
    moved = moved.transpose(2, 0, 3, 1, 4).reshape(
        local_b * pair_count * pair_dev, row_count * rows_dev
    )
    quarter_r = jnp.dot(moved, coeffs, precision=high, preferred_element_type=jnp.float32)
    return factor * jnp.einsum(
        "mn,bna->bma",
        weights,
        quarter_r.reshape(local_b, pair_count * pair_dev, orbitals),
        precision=high,
    )


def solution(mesh):
    in_specs = (P("pair", "row", None), P(), P())
    out_specs = P(("pair", "row"), None, None)
    return jax.shard_map(body, mesh=mesh, in_specs=in_specs, out_specs=out_specs, check_vma=False)
```

profile of v0, /device:TPU:1, one launch (start us, length us, event | category | flops | bytes accessed | tf_op | source)
XLA Modules:
  0.0 256.7 jit_solution(867813624517261005)
XLA Ops:
  0.0 8.5 %copy.8 = f32[32,25,1600]{2,1,0:T(8,128)} copy(f32[32,25,1600]{2,0,1:T(8,128)} %param.3) | data formatting | bytes 10240000 | tf_op args[0]
  8.5 5.8 %reshape.33 = f32[800,1600]{1,0:T(8,128)} reshape(f32[32,25,1600]{2,1,0:T(8,128)} %copy.8) | data formatting | bytes 10240000 | tf_op jit(solution)/shard_map/reshape | solution.py:32
  14.3 61.5 %fusion.19 = f32[1024,800]{1,0:T(8,128)} fusion(f32[1600,1024]{1,0:T(8,128)} %param.4, f32[800,1600]{1,0:T(8,128)} %reshape.33), kind=kOutput, calls=%fused_computation.25 | convolution fusion | flops 15728640000 | bytes 14950400 | tf_op jit(solution)/shard_map/dot_general | solution.py:35
  75.8 4.0 %reshape.34 = f32[4,1,64,1,3200]{4,2,0,3,1:T(8,128)S(1)} reshape(f32[1024,800]{1,0:T(8,128)} %fusion.19) | data formatting | bytes 6553600 | tf_op jit(solution)/shard_map/reshape | solution.py:38
  79.8 43.1 %all_to_all.21 = f32[4,1,64,1,3200]{4,2,3,1,0:T(8,128)S(1)} all-to-all(f32[4,1,64,1,3200]{4,2,3,1,0:T(8,128)S(1)} %bitcast.33), channel_id=1, replica_groups=mesh['pair'=4,'row'=64] {'pair'}, dimensions={0} | all-to-all | bytes 6553600 | tf_op jit(solution)/shard_map/all_to_all | solution.py:40
  122.8 0.0 copy-start
  122.8 3.8 %copy.11 = f32[1,4,64,1,3200]{4,1,3,0,2:T(4,128)} copy(f32[1,4,64,1,3200]{4,2,1,3,0:T(8,128)S(1)} %bitcast.32) | data formatting | bytes 6553600 | tf_op jit(solution)/shard_map/all_to_all | solution.py:40
  126.6 12.8 %all-to-all-start.1 = ((f32[1,4,64,1,3200]{4,1,3,0,2:T(4,128)}), f32[1,4,64,1,3200]{4,1,3,0,2:T(4,128)S(1)}, u32[]{:S(2)}, u32[]{:S(2)}) async-start(f32[1,4,64,1,3200]{4,1,3,0,2:T(4,128)} %copy.11), calls=%async_computation.1 | async-start | bytes 6553600 | tf_op jit(solution)/shard_map/all_to_all | solution.py:39
  139.4 0.0 copy-done
  139.4 2.0 fusion.3
  141.4 2.0 fusion.4
  143.3 68.9 %all-to-all-done.1 = f32[1,4,64,1,3200]{4,1,3,0,2:T(4,128)S(1)} async-done(((f32[1,4,64,1,3200]{4,1,3,0,2:T(4,128)}), f32[1,4,64,1,3200]{4,1,3,0,2:T(4,128)S(1)}, u32[]{:S(2)}, u32[]{:S(2)}) %all-to-all-start.1) | async-done | bytes 3276832 | tf_op jit(solution)/shard_map/all_to_all | solution.py:39
  212.3 5.2 %copy.12 = f32[1,4,64,1,3200]{2,1,4,3,0:T(4,128)} copy(f32[1,4,64,1,3200]{4,1,3,0,2:T(4,128)S(1)} %all-to-all-done.1) | data formatting | bytes 6553600 | tf_op jit(solution)/shard_map/all_to_all | solution.py:39
  217.5 13.1 %copy.13 = f32[4,4,32,64,25]{2,1,4,3,0:T(4,128)} copy(f32[4,4,32,64,25]{3,1,4,2,0:T(4,128)} %bitcast.31) | data formatting | bytes 6553600 | tf_op jit(solution)/shard_map/transpose | solution.py:47
  230.6 9.5 %dot_general.32 = f32[4,128,1600]{1,2,0:T(8,128)S(1)} reshape(f32[4,4,32,64,25]{2,1,4,3,0:T(4,128)} %copy.13) | data formatting | bytes 6553600 | tf_op jit(solution)/shard_map/dot_general | solution.py:50
  240.2 14.0 %fusion = f32[4,128,1024]{2,1,0:T(8,128)S(1)} fusion(f32[4,128,1600]{1,2,0:T(8,128)S(1)} %dot_general.32, f32[1600,1024]{1,0:T(8,128)} %param.4), kind=kOutput, calls=%fused_computation | convolution fusion | flops 10066329600 | bytes 11927552 | tf_op jit(solution)/shard_map/dot_general | solution.py:50
  254.2 2.3 fusion.2
  (2 shorter events, 0.0 us)
Async XLA Ops:
  122.8 16.5 %copy-start = (s32[128,2]{0,1:T(2,128)S(1)}, s32[128,2]{0,1:T(2,128)}, u32[]{:S(2)}) copy-start(s32[128,2]{0,1:T(2,128)} %param.5) | copy-start | bytes 3076
  126.6 85.7 %all-to-all-start.1 = ((f32[1,4,64,1,3200]{4,1,3,0,2:T(4,128)}), f32[1,4,64,1,3200]{4,1,3,0,2:T(4,128)S(1)}, u32[]{:S(2)}, u32[]{:S(2)}) async-start(f32[1,4,64,1,3200]{4,1,3,0,2:T(4,128)} %copy.11), calls=%async_computation.1 | async-start | bytes 6553600 | tf_op jit(solution)/shard_map/all_to_all | solution.py:39
where the time goes:
time: 258 us; the launch traced here: 257 us
  matrix products  81.8 us (32%)
  waiting for transfers between devices  68.9 us (27%)
  local copies, waits for them, and re-layouts  49.9 us (19%)
  blocking collectives  43.1 us (17%)
  starting transfers between devices  12.8 us (5%)
    all_to_all x1, waiting for transfers between devices, body(): lax.all_to_all(lax.all_to_all(packed, 'pair', split_axis=0, concat_axis=1...  68.9 us
    dot_general x1, matrix products, body(): lax.dot_general(coeffs, flat, (((0,), (1,)), ((), ())), precision=high, p...  61.5 us
    all_to_all x1, blocking collectives, body(): lax.all_to_all(packed, 'pair', split_axis=0, concat_axis=1, tiled=True)  43.1 us
    dot_general x1, matrix products, body(): jnp.dot(moved, coeffs, precision=high, preferred_element_type=jnp.float32)  14 us
    transpose x1, local copies, waits for them, and re-layouts, body(): moved.transpose(2, 0, 3, 1, 4)  13.1 us
    all_to_all x1, starting transfers between devices, body(): lax.all_to_all(lax.all_to_all(packed, 'pair', split_axis=0, concat_axis=1...  12.8 us
    dot_general x1, local copies, waits for them, and re-layouts, body(): jnp.dot(moved, coeffs, precision=high, preferred_element_type=jnp.float32)  9.54 us
    unnamed x3, local copies, waits for them, and re-layouts  8.46 us
  transfers between devices with their start and end apart: 1, of which 1 were waited for; matrix products, arithmetic and copies ran while one was open for 2% of the time, Pallas kernels for 0%

commit v1 on v0

v1 whole, which is shorter than its diff:
```python
import functools

import jax
import jax.numpy as jnp
from jax import lax
from jax.experimental import pallas as pl
from jax.experimental.pallas import tpu as pltpu
from jax.sharding import PartitionSpec as P

F32, BF16 = jnp.float32, jnp.bfloat16
NACT = 8
STARTS = [8 * i - i * (i - 1) // 2 for i in range(NACT)]
NSYM = 36
GROUP = 40
LANES = 128


def iota(shape, dim):
    return lax.broadcasted_iota(jnp.int32, shape, dim)


def split(x):
    hi = x.astype(BF16)
    return hi, (x - hi.astype(F32)).astype(BF16)


def dot(a, b, ca=1, cb=0, precision=None):
    return lax.dot_general(
        a, b, (((ca,), (cb,)), ((), ())), precision=precision, preferred_element_type=F32
    )


def dot3(a, b, ca=1, cb=0):
    (ah, al), (bh, bl) = a, b
    return dot(ah, bh, ca, cb) + (dot(ah, bl, ca, cb) + dot(al, bh, ca, cb))


def exact(a, b, ca=1, cb=0):
    return dot(a, b, ca, cb, lax.Precision.HIGHEST)


def first_second(m):
    i = jnp.zeros_like(m)
    start = jnp.zeros_like(m)
    for t in range(1, NACT):
        past = (m >= STARTS[t]).astype(jnp.int32)
        i = i + past
        start = start + past * (STARTS[t] - STARTS[t - 1])
    return i, m - start + i


def sym_index(ij):
    i, j = ij >> 3, ij & 7
    low, high = jnp.minimum(i, j), jnp.maximum(i, j)
    return 8 * low - ((low * (low - 1)) >> 1) + high - low


def make_weights(pair, pair_ref, c_ref, slim_ref, rows_ref):
    pairs_dev = rows_ref.shape[0] // 3
    slim_ref[...] = c_ref[:, 0:LANES]

    def pick(n, carry):
        p = pair_ref[pair * pairs_dev + n, 0]
        q = pair_ref[pair * pairs_dev + n, 1]
        rows_ref[pl.ds(n, 1), :] = slim_ref[pl.ds(p, 1), :]
        rows_ref[pl.ds(pairs_dev + n, 1), :] = slim_ref[pl.ds(q, 1), :]
        rows_ref[pl.ds(2 * pairs_dev + n, 1), :] = jnp.full((1, LANES), jnp.where(p != q, 1.0, 0.0), F32)
        return carry

    lax.fori_loop(0, pairs_dev, pick, 0)
    k, m = iota((LANES, LANES), 0), iota((LANES, LANES), 1)
    i, j = first_second(m)
    sel_i = jnp.where((k == i) & (m < NSYM), 1.0, 0.0).astype(F32)
    sel_j = jnp.where((k == j) & (m < NSYM), 1.0, 0.0).astype(F32)
    first, second, distinct = (rows_ref[t * pairs_dev : (t + 1) * pairs_dev, :] for t in range(3))
    weights = exact(first, sel_i) * exact(second, sel_j) + distinct * (
        exact(second, sel_i) * exact(first, sel_j)
    )
    spread = jnp.where(iota((pairs_dev, pairs_dev * 8), 0) == lax.rem(iota((pairs_dev, pairs_dev * 8), 1), pairs_dev), 1.0, 0.0).astype(F32)
    wide = exact(weights, spread, 0, 0)[:GROUP]
    column = lax.div(iota((GROUP, pairs_dev * 8), 1), pairs_dev)
    kron = jnp.concatenate([jnp.where(column == j, wide, 0.0) for j in range(8)], axis=0)
    row, m = iota((64, LANES), 0), iota((64, LANES), 1)
    last = jnp.where(((row & 7) < 5) & (m == 5 * (row >> 3) + (row & 7)), 1.0, 0.0).astype(F32)
    return split(kron), split(exact(last, weights, 1, 1))


def sum_pairs(x_ref, kron, last, vh_ref, vl_ref, s0, width):
    pairs_dev = x_ref.shape[1]
    cols = pl.ds(s0, width)
    parts = [
        dot3(kron, split(x_ref[8 * q : 8 * q + 8, :, cols].reshape(pairs_dev * 8, width))) for q in range(3)
    ]
    tail = dot3(last, split(x_ref[24, :, cols]))
    for j in range(8):
        block = jnp.concatenate(
            [part[GROUP * j : GROUP * (j + 1)] for part in parts] + [tail[8 * j : 8 * j + 8]], axis=0
        )
        hi, lo = split(block)
        vh_ref[LANES * j : LANES * (j + 1), cols] = hi
        vl_ref[LANES * j : LANES * (j + 1), cols] = lo


def sum_all_pairs(x_ref, kron, last, vh_ref, vl_ref):
    basis = x_ref.shape[2]
    step = 256
    whole = basis // step

    def some(t, carry):
        sum_pairs(x_ref, kron, last, vh_ref, vl_ref, pl.multiple_of(t * step, step), step)
        return carry

    lax.fori_loop(0, whole, some, 0)
    if basis % step:
        sum_pairs(x_ref, kron, last, vh_ref, vl_ref, whole * step, basis % step)


def split_coeffs(c_ref, ch_ref, cl_ref):
    step = 64

    def some(t, carry):
        rows = pl.ds(pl.multiple_of(t * step, step), step)
        hi, lo = split(c_ref[rows, :])
        ch_ref[rows, :] = hi
        cl_ref[rows, :] = lo
        return carry

    lax.fori_loop(0, c_ref.shape[0] // step, some, 0)


def contract_s(v, c):
    return dot3(v, c)


def arrange_coeffs(c_ref, qh_ref, ql_ref, th_ref, tl_ref, sources):
    rows_dev = c_ref.shape[0] // sources
    for s in range(0, sources, 2):
        for q in range(3):
            block = jnp.concatenate(
                [c_ref[(s + u) * rows_dev + 8 * q : (s + u) * rows_dev + 8 * q + 8, :] for u in range(2)], axis=0
            )
            hi, lo = split(block)
            qh_ref[q, 8 * s : 8 * s + 16, :] = hi
            ql_ref[q, 8 * s : 8 * s + 16, :] = lo
    for s in range(0, sources, 16):
        block = jnp.concatenate(
            [c_ref[(s + u) * rows_dev + 24 : (s + u) * rows_dev + 25, :] for u in range(16)], axis=0
        )
        hi, lo = split(block)
        th_ref[s : s + 16, :] = hi
        tl_ref[s : s + 16, :] = lo


def select(q, local_b):
    shape = (local_b * 64, local_b * LANES)
    row, col = iota(shape, 0), iota(shape, 1)
    sym = sym_index(row & 63)
    lane = GROUP * q + sym if q < 3 else 120 + sym - 5 * ((sym * 52) >> 8)
    return jnp.where(((row >> 6) == (col >> 7)) & ((col & 127) == lane), 1.0, 0.0).astype(BF16)


def unfold(x, q, local_b):
    pick = select(q, local_b)
    return [dot(pick, part, 1, 1).astype(BF16) for part in x]


def contract_r(x, qh_ref, ql_ref, th_ref, tl_ref, local_b):
    total = None
    for q in range(3):
        term = dot3(unfold(x, q, local_b), (qh_ref[q], ql_ref[q]))
        total = term if total is None else total + term
    y = unfold(x, 3, local_b)
    count = y[0].shape[1]
    row, col = iota(y[0].shape, 0), iota(y[0].shape, 1)
    keep = ((sym_index(row & 63) * 52) >> 8) == (col & 7)
    gather = jnp.where((iota((count, count // 8), 0) >> 3) == iota((count, count // 8), 1), 1.0, 0.0).astype(BF16)
    y = [dot(jnp.where(keep, part, jnp.zeros_like(part)), gather).astype(BF16) for part in y]
    return total + dot3(y, (th_ref[...], tl_ref[...]))

VMEM = pl.BlockSpec(memory_space=pltpu.VMEM)
SMEM = pl.BlockSpec(memory_space=pltpu.SMEM)
LIMIT = 60 * 1024 * 1024


def local_kernel(pair_ref, x_ref, c_ref, z_ref, slim_ref, rows_ref, vh_ref, vl_ref, ch_ref, cl_ref):
    kron, last = make_weights(lax.axis_index("pair"), pair_ref, c_ref, slim_ref, rows_ref)
    split_coeffs(c_ref, ch_ref, cl_ref)
    sum_all_pairs(x_ref, kron, last, vh_ref, vl_ref)
    step = 256

    def some(t, carry):
        cols = pl.ds(pl.multiple_of(t * step, step), step)
        z = contract_s((vh_ref[...], vl_ref[...]), (ch_ref[:, cols], cl_ref[:, cols]))
        for j in range(8):
            z_ref[pl.ds(pl.multiple_of(t * step * 8, step * 8) + j, step, stride=8), :] = z[LANES * j : LANES * (j + 1)].T
        return carry

    lax.fori_loop(0, c_ref.shape[1] // step, some, 0)


def local_part(integrals, coeffs, pair_list):
    pairs_dev, rows_dev, basis = integrals.shape
    orbitals = coeffs.shape[1]
    return pl.pallas_call(
        local_kernel,
        out_shape=jax.ShapeDtypeStruct((orbitals * 8, LANES), F32),
        in_specs=[SMEM, VMEM, VMEM],
        out_specs=VMEM,
        scratch_shapes=[
            pltpu.VMEM((basis, LANES), F32),
            pltpu.VMEM((3 * pairs_dev, LANES), F32),
            pltpu.VMEM((8 * LANES, basis), BF16),
            pltpu.VMEM((8 * LANES, basis), BF16),
            pltpu.VMEM((basis, orbitals), BF16),
            pltpu.VMEM((basis, orbitals), BF16),
        ],
        compiler_params=pltpu.CompilerParams(vmem_limit_bytes=LIMIT),
        name="sum_s_and_pairs",
    )(pair_list, integrals.transpose(1, 0, 2), coeffs)


def final_kernel(factor, x_ref, c_ref, o_ref, qh_ref, ql_ref, th_ref, tl_ref):
    sources, local_b = x_ref.shape[:2]
    arrange_coeffs(c_ref, qh_ref, ql_ref, th_ref, tl_ref, sources)
    x = split(jnp.concatenate([x_ref[:, b].reshape(sources * 8, LANES) for b in range(local_b)], axis=1))
    out = factor * contract_r(x, qh_ref, ql_ref, th_ref, tl_ref, local_b)
    o_ref[...] = out.reshape(o_ref.shape)


def final_part(x, coeffs, factor):
    sources, local_b = x.shape[:2]
    orbitals = coeffs.shape[1]
    return pl.pallas_call(
        functools.partial(final_kernel, factor),
        out_shape=jax.ShapeDtypeStruct((local_b, 64, orbitals), F32),
        in_specs=[VMEM, VMEM],
        out_specs=VMEM,
        scratch_shapes=[
            pltpu.VMEM((3, sources * 8, orbitals), BF16),
            pltpu.VMEM((3, sources * 8, orbitals), BF16),
            pltpu.VMEM((sources, orbitals), BF16),
            pltpu.VMEM((sources, orbitals), BF16),
        ],
        compiler_params=pltpu.CompilerParams(vmem_limit_bytes=LIMIT),
        name="sum_r",
    )(x, coeffs)


def body(integrals, coeffs, pair_list):
    basis, orbitals = coeffs.shape
    pair_count, row_count = lax.axis_size("pair"), lax.axis_size("row")
    local_b = orbitals // (pair_count * row_count)
    factor = basis / (2.0 * pair_list.shape[0]) ** 0.5
    z = local_part(integrals, coeffs, pair_list)
    z = lax.psum_scatter(z, "pair", scatter_dimension=0, tiled=True)
    z = z.reshape(row_count, local_b, 8, LANES)
    z = lax.all_to_all(z, "row", split_axis=0, concat_axis=0, tiled=True)
    return final_part(z, coeffs, factor)


def solution(mesh):
    in_specs = (P("pair", "row", None), P(), P())
    out_specs = P(("pair", "row"), None, None)
    return jax.shard_map(body, mesh=mesh, in_specs=in_specs, out_specs=out_specs, check_vma=False)
```

time: 258 us -> 144 us (0.56)
  matrix products: 81.8 us -> 0 us
  local copies, waits for them, and re-layouts: 49.9 us -> 1.41 us
  Pallas kernels: 0 us -> 34.1 us
  waiting for transfers between devices: 68.9 us -> 52.1 us
  between operations: 0.29 us -> 13.4 us
  starting transfers between devices: 12.8 us -> 0.01 us
  blocking collectives: 43.1 us -> 40.5 us
    dot_general x5 -> x0, matrix products: 81.8 us -> none  [the longest x1 61.5 us: body(): lax.dot_general(coeffs, flat, (((0,), (1,)), ((), ())), precision=high, p...]
    all_to_all x1 -> x0, waiting for transfers between devices: 68.9 us -> none  [body(): lax.all_to_all(lax.all_to_all(packed, 'pair', split_axis=0, concat_axis=1...]
    reduce_scatter x0 -> x1, waiting for transfers between devices: none -> 52.1 us  [body(): z = lax.psum_scatter(z, 'pair', scatter_dimension=0, tiled=True)]
    pallas_call x0 -> x2, Pallas kernels: none -> 34.1 us  [the longest x1 25 us: local_part(): pl.pallas_call(local_kernel, out_shape=jax.ShapeDtypeStruct((orbitals * 8...]
    transpose x1 -> x0, local copies, waits for them, and re-layouts: 13.1 us -> none  [body(): moved.transpose(2, 0, 3, 1, 4)]
    all_to_all x1 -> x0, starting transfers between devices: 12.8 us -> none  [body(): lax.all_to_all(lax.all_to_all(packed, 'pair', split_axis=0, concat_axis=1...]
    reshape x2 -> x0, local copies, waits for them, and re-layouts: 9.76 us -> none  [the longest x1 5.8 us: body(): flat = integrals.reshape(pair_dev * rows_dev, basis)]
    dot_general x1 -> x0, local copies, waits for them, and re-layouts: 9.54 us -> none  [body(): jnp.dot(moved, coeffs, precision=high, preferred_element_type=jnp.float32)]
  transfers between devices with their start and end apart: 1 -> 1, of which waited for: 1 -> 1; matrix products, arithmetic and copies ran while one was open for 2% -> 0% of each run, Pallas kernels for 0% -> 0%
where the time goes in v1:
time: 144 us; the launch traced here: 142 us
  waiting for transfers between devices  52.1 us (36%)
  blocking collectives  40.5 us (28%)
  Pallas kernels  34.1 us (24%)
  between operations  13.4 us (9%)
    reduce_scatter x1, waiting for transfers between devices, body(): z = lax.psum_scatter(z, 'pair', scatter_dimension=0, tiled=True)  52.1 us
    all_to_all x1, blocking collectives, body(): z = lax.all_to_all(z, 'row', split_axis=0, concat_axis=0, tiled=True)  40.5 us
    pallas_call x1, Pallas kernels, local_part(): pl.pallas_call(local_kernel, out_shape=jax.ShapeDtypeStruct((orbitals * 8...  25 us
    pallas_call x1, Pallas kernels, final_part(): pl.pallas_call(functools.partial(final_kernel, factor), out_shape=jax.Sha...  9.1 us
  transfers between devices with their start and end apart: 1, of which 1 were waited for; matrix products, arithmetic and copies ran while one was open for 0% of the time, Pallas kernels for 0%

profile of v1, /device:TPU:1, one launch (start us, length us, event | category | flops | bytes accessed | tf_op | source)
XLA Modules:
  0.0 141.5 jit_solution(15487308682357750859)
XLA Ops:
  6.5 0.0 reduce-scatter.2.cloned.1.call-start
  6.5 1.4 copy.4.pair_ref
  8.0 25.0 %sum_s_and_pairs.1 = f32[8192,128]{1,0:T(8,128)} custom-call(s32[128,2]{1,0:T(8,128)} %copy.4.pair_ref, f32[25,32,1600]{2,1,0:T(8,128)} %bitcast.2, f32[1600,1024]{1,0:T(8,128)} %c_ref.3), custom_call_target="tpu_custom_call" | custom-call | tf_op jit(solution)/shard_map/sum_s_and_pairs/pallas_call | solution.py:204
  33.0 0.0 reduce-scatter.2.cloned.1.call-update
  33.0 52.1 %reduce-scatter.2.cloned.1.call-done = f32[2048,128]{1,0:T(8,128)} async-done(((f32[8192,128]{1,0:T(8,128)}), f32[2048,128]{1,0:T(8,128)}) %reduce-scatter.2.cloned.1.call-update) | async-done | bytes 1048592 | tf_op jit(solution)/shard_map/reduce_scatter | solution.py:255
  85.1 40.5 %all_to_all.5.x_ref = f32[64,4,8,128]{3,2,1,0:T(8,128)} all-to-all(f32[64,4,8,128]{3,2,1,0:T(8,128)} %bitcast.3), channel_id=1, replica_groups=mesh['pair'=4,'row'=64] {'row'}, dimensions={0} | all-to-all | bytes 2097152 | tf_op jit(solution)/shard_map/all_to_all | solution.py:257
  125.6 9.1 %sum_r.1 = f32[4,64,1024]{2,1,0:T(8,128)} custom-call(f32[64,4,8,128]{3,2,1,0:T(8,128)} %all_to_all.5.x_ref, f32[1600,1024]{1,0:T(8,128)} %c_ref.3), custom_call_target="tpu_custom_call" | custom-call | tf_op jit(solution)/shard_map/sum_r/pallas_call | solution.py:233
Async XLA Ops:
  6.5 78.6 %reduce-scatter.2.cloned.1.call-start = ((), (), s32[]{:S(2)}) async-start(), calls=%async_computation.2 | async-start | bytes 5242880 | tf_op jit(solution)/shard_map/reduce_scatter | solution.py:255
Sparse Core Ops, SparseCore 0:
  33.1 51.9 reduce-scatter.1

commit v2 on v1

--- a/solution.py
+++ b/solution.py
@@ -55,9 +55,8 @@
     return 8 * low - ((low * (low - 1)) >> 1) + high - low
 
 
-def make_weights(pair, pair_ref, c_ref, slim_ref, rows_ref):
+def make_weights(pair, pair_ref, slim_ref, rows_ref):
     pairs_dev = rows_ref.shape[0] // 3
-    slim_ref[...] = c_ref[:, 0:LANES]
 
     def pick(n, carry):
         p = pair_ref[pair * pairs_dev + n, 0]
@@ -101,31 +100,28 @@
         vl_ref[LANES * j : LANES * (j + 1), cols] = lo
 
 
-def sum_all_pairs(x_ref, kron, last, vh_ref, vl_ref):
+def split_coeffs(c_ref, ch_ref, cl_ref, start, size):
+    rows = pl.ds(start, size)
+    hi, lo = split(c_ref[rows, :])
+    ch_ref[rows, :] = hi
+    cl_ref[rows, :] = lo
+
+
+def sum_all_pairs(x_ref, kron, last, vh_ref, vl_ref, c_ref, ch_ref, cl_ref):
     basis = x_ref.shape[2]
     step = 256
     whole = basis // step
 
     def some(t, carry):
-        sum_pairs(x_ref, kron, last, vh_ref, vl_ref, pl.multiple_of(t * step, step), step)
+        start = pl.multiple_of(t * step, step)
+        split_coeffs(c_ref, ch_ref, cl_ref, start, step)
+        sum_pairs(x_ref, kron, last, vh_ref, vl_ref, start, step)
         return carry
 
     lax.fori_loop(0, whole, some, 0)
     if basis % step:
+        split_coeffs(c_ref, ch_ref, cl_ref, whole * step, basis % step)
         sum_pairs(x_ref, kron, last, vh_ref, vl_ref, whole * step, basis % step)
-
-
-def split_coeffs(c_ref, ch_ref, cl_ref):
-    step = 64
-
-    def some(t, carry):
-        rows = pl.ds(pl.multiple_of(t * step, step), step)
-        hi, lo = split(c_ref[rows, :])
-        ch_ref[rows, :] = hi
-        cl_ref[rows, :] = lo
-        return carry
-
-    lax.fori_loop(0, c_ref.shape[0] // step, some, 0)
 
 
 def contract_s(v, c):
@@ -164,98 +160,215 @@
     return [dot(pick, part, 1, 1).astype(BF16) for part in x]
 
 
-def contract_r(x, qh_ref, ql_ref, th_ref, tl_ref, local_b):
+def contract_r(x, qh_ref, ql_ref, th_ref, tl_ref, part, sources, local_b):
+    rows = pl.ds(pl.multiple_of(part * (sources * 8), sources * 8), sources * 8)
     total = None
     for q in range(3):
-        term = dot3(unfold(x, q, local_b), (qh_ref[q], ql_ref[q]))
+        term = dot3(unfold(x, q, local_b), (qh_ref[q, rows, :], ql_ref[q, rows, :]))
         total = term if total is None else total + term
     y = unfold(x, 3, local_b)
     count = y[0].shape[1]
     row, col = iota(y[0].shape, 0), iota(y[0].shape, 1)
     keep = ((sym_index(row & 63) * 52) >> 8) == (col & 7)
-    gather = jnp.where((iota((count, count // 8), 0) >> 3) == iota((count, count // 8), 1), 1.0, 0.0).astype(BF16)
-    y = [dot(jnp.where(keep, part, jnp.zeros_like(part)), gather).astype(BF16) for part in y]
-    return total + dot3(y, (th_ref[...], tl_ref[...]))
-
-VMEM = pl.BlockSpec(memory_space=pltpu.VMEM)
+    gather = jnp.where((iota((count, sources), 0) >> 3) == iota((count, sources), 1), 1.0, 0.0).astype(BF16)
+    y = [dot(jnp.where(keep, half, jnp.zeros_like(half)), gather).astype(BF16) for half in y]
+    rows = pl.ds(pl.multiple_of(part * sources, sources), sources)
+    return total + dot3(y, (th_ref[rows, :], tl_ref[rows, :]))
+
 SMEM = pl.BlockSpec(memory_space=pltpu.SMEM)
-LIMIT = 60 * 1024 * 1024
-
-
-def local_kernel(pair_ref, x_ref, c_ref, z_ref, slim_ref, rows_ref, vh_ref, vl_ref, ch_ref, cl_ref):
-    kron, last = make_weights(lax.axis_index("pair"), pair_ref, c_ref, slim_ref, rows_ref)
-    split_coeffs(c_ref, ch_ref, cl_ref)
-    sum_all_pairs(x_ref, kron, last, vh_ref, vl_ref)
-    step = 256
-
-    def some(t, carry):
-        cols = pl.ds(pl.multiple_of(t * step, step), step)
-        z = contract_s((vh_ref[...], vl_ref[...]), (ch_ref[:, cols], cl_ref[:, cols]))
+ANY = pl.BlockSpec(memory_space=pl.ANY)
+LIMIT = 62 * 1024 * 1024
+MESH = pl.DeviceIdType.MESH
+CORES, Y_LO, Y_HI, X, Z = 2, 2, 2, 4, 8
+PLANE = X * Z
+SIDE = 128
+ROWS = SIDE * 8
+PIECE = ROWS // X
+MESSAGE = ROWS // PLANE
+
+
+def copy_bytes_of(ref, sem):
+    pltpu.make_async_copy(ref, ref, sem).wait()
+
+
+def kernel(factor, pair_ref, x_hbm, c_hbm, o_ref, x_ref, c_ref, slim_ref, rows_ref, vh_ref, vl_ref, ch_ref, cl_ref,
+           qh_ref, ql_ref, th_ref, tl_ref, away_ref, here_ref, core_ref, side_ref, got_ref,
+           load_sem, core_send, core_recv, side_send, side_recv, put_send, put_recv):
+    pair, row = lax.axis_index("pair"), lax.axis_index("row")
+    y_lo, core = pair // CORES, pair % CORES
+    y_hi, spot = row // PLANE, row % PLANE
+    x = spot // Z
+    other_core = (y_lo * CORES + 1 - core, row)
+    other_side = ((1 - y_lo) * CORES + core, row)
+    corner = (1 - y_lo) * CORES + core, 1 - y_hi
+
+    slim_load = pltpu.make_async_copy(c_hbm.at[:, 0:LANES], slim_ref, load_sem.at[0])
+    x_load = pltpu.make_async_copy(x_hbm, x_ref, load_sem.at[1])
+    c_load = pltpu.make_async_copy(c_hbm, c_ref, load_sem.at[2])
+    slim_load.start()
+    x_load.start()
+    c_load.start()
+
+    barrier = pltpu.get_barrier_semaphore()
+    pl.semaphore_signal(barrier, inc=1, device_id=other_core, device_id_type=MESH)
+    pl.semaphore_signal(barrier, inc=1, device_id=other_side, device_id_type=MESH)
+
+    def greet(t, carry):
+        pl.semaphore_signal(
+            barrier, inc=1, device_id=(corner[0], corner[1] * PLANE + t), device_id_type=MESH
+        )
+        return carry
+
+    def greet_own(t, carry):
+        pl.semaphore_signal(
+            barrier, inc=1, device_id=(pair, y_hi * PLANE + (spot + t) % PLANE), device_id_type=MESH
+        )
+        return carry
+
+    lax.fori_loop(0, PLANE, greet, 0)
+    lax.fori_loop(1, PLANE, greet_own, 0)
+
+    slim_load.wait()
+    kron, last = make_weights(pair, pair_ref, slim_ref, rows_ref)
+    x_load.wait()
+    c_load.wait()
+    sum_all_pairs(x_ref, kron, last, vh_ref, vl_ref, c_ref, ch_ref, cl_ref)
+    pl.semaphore_wait(barrier, 2 * PLANE + 1)
+
+    planes = [(y_lo, 1 - y_hi), (1 - y_lo, y_hi), (1 - y_lo, 1 - y_hi), (y_lo, y_hi)]
+
+    def block(ref, k, start=0, size=ROWS):
+        return ref.at[pl.ds(k * ROWS + start, size), :]
+
+    def core_copy(k):
+        return pltpu.make_async_remote_copy(
+            block(away_ref, k), block(core_ref, k), core_send.at[k], core_recv.at[k],
+            device_id=other_core, device_id_type=MESH)
+
+    def spot_x(i):
+        return (x + i) % X
+
+    def side_copy(k, i):
+        start = spot_x(i) * PIECE
+        return pltpu.make_async_remote_copy(
+            block(here_ref, k, start, PIECE), block(side_ref, k, start, PIECE), side_send.at[k, i], side_recv.at[k, i],
+            device_id=other_side, device_id_type=MESH)
+
+    def compute(k):
+        y_lo_to, y_hi_to = planes[k]
+        away = (y_lo_to * CORES + 1 - core) * Y_HI + y_hi_to
+        here = (y_lo_to * CORES + core) * Y_HI + y_hi_to
+        cols = [pl.ds(pl.multiple_of(side * SIDE, SIDE), SIDE) for side in (away, here)]
+        c = [jnp.concatenate([ref[:, col] for col in cols], axis=1) for ref in (ch_ref, cl_ref)]
+        z = contract_s((vh_ref[...], vl_ref[...]), c)
         for j in range(8):
-            z_ref[pl.ds(pl.multiple_of(t * step * 8, step * 8) + j, step, stride=8), :] = z[LANES * j : LANES * (j + 1)].T
-        return carry
-
-    lax.fori_loop(0, c_ref.shape[1] // step, some, 0)
-
-
-def local_part(integrals, coeffs, pair_list):
+            part = z[LANES * j : LANES * (j + 1)].T
+            away_ref[pl.ds(k * ROWS + j, SIDE, stride=8), :] = part[:SIDE]
+            here_ref[pl.ds(k * ROWS + j, SIDE, stride=8), :] = part[SIDE:]
+        core_copy(k).start()
+
+    def add_core(k):
+        core_copy(k).wait_recv()
+        here = block(here_ref, k)
+        here[...] += block(core_ref, k)[...]
+
+    def to_side(k):
+        add_core(k)
+        for i in range(X):
+            side_copy(k, i).start()
+
+    def put(u, t, copied_to):
+        pltpu.make_async_remote_copy(
+            block(here_ref, 2 + u, t * MESSAGE, MESSAGE), got_ref.at[row], put_send.at[u], put_recv.at[u],
+            device_id=(copied_to[0], copied_to[1] * PLANE + t), device_id_type=MESH).start()
+
+    def spread(u, copied_to):
+        for i in range(X):
+            side_copy(u, i).wait_recv()
+            start = spot_x(i) * PIECE
+            here = block(here_ref, 2 + u, start, PIECE)
+            here[...] += block(side_ref, u, start, PIECE)[...]
+            own = u == 1 and i == 0
+
+            def one(t, carry):
+                put(u, spot_x(i) * Z + (spot + t) % Z, copied_to)
+                return carry
+
+            lax.fori_loop(1 if own else 0, Z, one, 0)
+            if own:
+                pltpu.make_async_copy(
+                    block(here_ref, 2 + u, spot * MESSAGE, MESSAGE), got_ref.at[row], put_recv.at[u]).start()
+
+    def take(u, y_hi_from):
+        got = got_ref.at[pl.ds(y_hi_from * PLANE, PLANE)]
+        copy_bytes_of(got, put_recv.at[u])
+        local_b = MESSAGE // 8
+        blocks = split(jnp.concatenate([got[:, 8 * b : 8 * b + 8, :].reshape(PLANE * 8, LANES) for b in range(local_b)], axis=1))
+        return contract_r(blocks, qh_ref, ql_ref, th_ref, tl_ref, y_hi_from, PLANE, local_b)
+
+    compute(0)
+    compute(1)
+    to_side(0)
+    compute(2)
+    to_side(1)
+    compute(3)
+    add_core(2)
+    add_core(3)
+    spread(0, corner)
+    arrange_coeffs(c_ref, qh_ref, ql_ref, th_ref, tl_ref, Y_HI * PLANE)
+    spread(1, (pair, y_hi))
+    total = take(0, 1 - y_hi)
+    o_ref[...] = factor * (total + take(1, y_hi)).reshape(o_ref.shape)
+
+    for k in range(4):
+        core_copy(k).wait_send()
+    for k in range(2):
+        for i in range(X):
+            side_copy(k, i).wait_send()
+    copy_bytes_of(block(here_ref, 2), put_send.at[0])
+    copy_bytes_of(block(here_ref, 3, 0, ROWS - MESSAGE), put_send.at[1])
+
+
+def body(integrals, coeffs, pair_list):
     pairs_dev, rows_dev, basis = integrals.shape
     orbitals = coeffs.shape[1]
+    factor = basis / (2.0 * pair_list.shape[0]) ** 0.5
+    sources = Y_HI * PLANE
     return pl.pallas_call(
-        local_kernel,
-        out_shape=jax.ShapeDtypeStruct((orbitals * 8, LANES), F32),
-        in_specs=[SMEM, VMEM, VMEM],
-        out_specs=VMEM,
+        functools.partial(kernel, factor),
+        out_shape=jax.ShapeDtypeStruct((SIDE // PLANE, NACT * NACT, orbitals), F32),
+        in_specs=[SMEM, ANY, ANY],
+        out_specs=pl.BlockSpec(memory_space=pltpu.VMEM),
         scratch_shapes=[
+            pltpu.VMEM((rows_dev, pairs_dev, basis), F32),
+            pltpu.VMEM((basis, orbitals), F32),
             pltpu.VMEM((basis, LANES), F32),
             pltpu.VMEM((3 * pairs_dev, LANES), F32),
             pltpu.VMEM((8 * LANES, basis), BF16),
             pltpu.VMEM((8 * LANES, basis), BF16),
             pltpu.VMEM((basis, orbitals), BF16),
             pltpu.VMEM((basis, orbitals), BF16),
-        ],
-        compiler_params=pltpu.CompilerParams(vmem_limit_bytes=LIMIT),
-        name="sum_s_and_pairs",
-    )(pair_list, integrals.transpose(1, 0, 2), coeffs)
-
-
-def final_kernel(factor, x_ref, c_ref, o_ref, qh_ref, ql_ref, th_ref, tl_ref):
-    sources, local_b = x_ref.shape[:2]
-    arrange_coeffs(c_ref, qh_ref, ql_ref, th_ref, tl_ref, sources)
-    x = split(jnp.concatenate([x_ref[:, b].reshape(sources * 8, LANES) for b in range(local_b)], axis=1))
-    out = factor * contract_r(x, qh_ref, ql_ref, th_ref, tl_ref, local_b)
-    o_ref[...] = out.reshape(o_ref.shape)
-
-
-def final_part(x, coeffs, factor):
-    sources, local_b = x.shape[:2]
-    orbitals = coeffs.shape[1]
-    return pl.pallas_call(
-        functools.partial(final_kernel, factor),
-        out_shape=jax.ShapeDtypeStruct((local_b, 64, orbitals), F32),
-        in_specs=[VMEM, VMEM],
-        out_specs=VMEM,
-        scratch_shapes=[
             pltpu.VMEM((3, sources * 8, orbitals), BF16),
             pltpu.VMEM((3, sources * 8, orbitals), BF16),
             pltpu.VMEM((sources, orbitals), BF16),
             pltpu.VMEM((sources, orbitals), BF16),
+            pltpu.VMEM((4 * ROWS, LANES), F32),
+            pltpu.VMEM((4 * ROWS, LANES), F32),
+            pltpu.VMEM((4 * ROWS, LANES), F32),
+            pltpu.VMEM((2 * ROWS, LANES), F32),
+            pltpu.VMEM((sources, MESSAGE, LANES), F32),
+            pltpu.SemaphoreType.DMA((3,)),
+            pltpu.SemaphoreType.DMA((4,)),
+            pltpu.SemaphoreType.DMA((4,)),
+            pltpu.SemaphoreType.DMA((2, X)),
+            pltpu.SemaphoreType.DMA((2, X)),
+            pltpu.SemaphoreType.DMA((2,)),
+            pltpu.SemaphoreType.DMA((2,)),
         ],
-        compiler_params=pltpu.CompilerParams(vmem_limit_bytes=LIMIT),
-        name="sum_r",
-    )(x, coeffs)
-
-
-def body(integrals, coeffs, pair_list):
-    basis, orbitals = coeffs.shape
-    pair_count, row_count = lax.axis_size("pair"), lax.axis_size("row")
-    local_b = orbitals // (pair_count * row_count)
-    factor = basis / (2.0 * pair_list.shape[0]) ** 0.5
-    z = local_part(integrals, coeffs, pair_list)
-    z = lax.psum_scatter(z, "pair", scatter_dimension=0, tiled=True)
-    z = z.reshape(row_count, local_b, 8, LANES)
-    z = lax.all_to_all(z, "row", split_axis=0, concat_axis=0, tiled=True)
-    return final_part(z, coeffs, factor)
+        compiler_params=pltpu.CompilerParams(vmem_limit_bytes=LIMIT, collective_id=0, has_side_effects=True),
+        cost_estimate=pl.CostEstimate(flops=15_000_000_000, bytes_accessed=14_000_000, transcendentals=0),
+        name="transform",
+    )(pair_list, integrals.transpose(1, 0, 2), coeffs)
 
 
 def solution(mesh):

time: 144 us -> 78.2 us (0.54); the launches traced: 142 us -> 78 us
  waiting for transfers between devices: 52.1 us -> 0 us
  blocking collectives: 40.5 us -> 0 us
  Pallas kernels: 34.1 us -> 74.3 us
  between operations: 13.4 us -> 0.01 us
  local copies, waits for them, and re-layouts: 1.41 us -> 3.72 us
    reduce_scatter x1 -> x0, waiting for transfers between devices: 52.1 us -> none  [body(): z = lax.psum_scatter(z, 'pair', scatter_dimension=0, tiled=True)]
    all_to_all x1 -> x0, blocking collectives: 40.5 us -> none  [body(): z = lax.all_to_all(z, 'row', split_axis=0, concat_axis=0, tiled=True)]
    pallas_call x2 -> x1, Pallas kernels: 34.1 us -> 74.3 us  [body(): pl.pallas_call(functools.partial(kernel, factor), out_shape=jax.ShapeDtyp...]
    unnamed x1 -> x2, local copies, waits for them, and re-layouts: 1.41 us -> 3.72 us
  transfers between devices with their start and end apart: 1 -> 0, of which waited for: 1 -> 0; matrix products, arithmetic and copies ran while one was open for 0% -> 0% of each run, Pallas kernels for 0% -> 0%
where the time goes in v2:
time: 78.2 us; the launch traced here: 78 us
  Pallas kernels  74.3 us (95%)
  local copies, waits for them, and re-layouts  3.72 us (5%)
    pallas_call x1, Pallas kernels, body(): pl.pallas_call(functools.partial(kernel, factor), out_shape=jax.ShapeDtyp...  74.3 us
    unnamed x2, local copies, waits for them, and re-layouts  3.72 us

profile of v2, /device:TPU:1, one launch (start us, length us, event | category | flops | bytes accessed | tf_op | source)
XLA Modules:
  0.0 78.0 jit_solution(3426193733977650672)
XLA Ops:
  0.0 1.4 %copy.4.pair_ref = s32[128,2]{1,0:T(8,128)} copy(s32[128,2]{0,1:T(2,128)} %param.5) | data formatting | bytes 2048 | tf_op args[2]
  1.4 74.3 %transform.1 = f32[4,64,1024]{2,1,0:T(8,128)} custom-call(s32[128,2]{1,0:T(8,128)} %copy.4.pair_ref, f32[25,32,1600]{2,1,0:T(8,128)} %bitcast.1, f32[1600,1024]{1,0:T(8,128)} %c_hbm.1), custom_call_target="tpu_custom_call" | custom-call | flops 15000000512 | bytes 14000000 | tf_op jit(solution)/shard_map/transform/pallas_call | solution.py:337
  75.7 2.3 %copy.6 = f32[4,64,1024]{2,1,0:T(8,128)} copy(f32[4,64,1024]{2,1,0:T(8,128)} %transform.1) | data formatting | bytes 2097152

commit v3 on v2

--- a/solution.py
+++ b/solution.py
@@ -13,6 +13,7 @@
 NSYM = 36
 GROUP = 40
 LANES = 128
+STEP = 256
 
 
 def iota(shape, dim):
@@ -59,8 +60,8 @@
     pairs_dev = rows_ref.shape[0] // 3
 
     def pick(n, carry):
-        p = pair_ref[pair * pairs_dev + n, 0]
-        q = pair_ref[pair * pairs_dev + n, 1]
+        p = pair_ref[0, pair * pairs_dev + n]
+        q = pair_ref[1, pair * pairs_dev + n]
         rows_ref[pl.ds(n, 1), :] = slim_ref[pl.ds(p, 1), :]
         rows_ref[pl.ds(pairs_dev + n, 1), :] = slim_ref[pl.ds(q, 1), :]
         rows_ref[pl.ds(2 * pairs_dev + n, 1), :] = jnp.full((1, LANES), jnp.where(p != q, 1.0, 0.0), F32)
@@ -107,21 +108,8 @@
     cl_ref[rows, :] = lo
 
 
-def sum_all_pairs(x_ref, kron, last, vh_ref, vl_ref, c_ref, ch_ref, cl_ref):
-    basis = x_ref.shape[2]
-    step = 256
-    whole = basis // step
-
-    def some(t, carry):
-        start = pl.multiple_of(t * step, step)
-        split_coeffs(c_ref, ch_ref, cl_ref, start, step)
-        sum_pairs(x_ref, kron, last, vh_ref, vl_ref, start, step)
-        return carry
-
-    lax.fori_loop(0, whole, some, 0)
-    if basis % step:
-        split_coeffs(c_ref, ch_ref, cl_ref, whole * step, basis % step)
-        sum_pairs(x_ref, kron, last, vh_ref, vl_ref, whole * step, basis % step)
+def load_steps(basis):
+    return [(start, min(STEP, basis - start)) for start in range(0, basis, STEP)]
 
 
 def contract_s(v, c):
@@ -183,7 +171,6 @@
 PLANE = X * Z
 SIDE = 128
 ROWS = SIDE * 8
-PIECE = ROWS // X
 MESSAGE = ROWS // PLANE
 
 
@@ -192,7 +179,7 @@
 
 
 def kernel(factor, pair_ref, x_hbm, c_hbm, o_ref, x_ref, c_ref, slim_ref, rows_ref, vh_ref, vl_ref, ch_ref, cl_ref,
-           qh_ref, ql_ref, th_ref, tl_ref, away_ref, here_ref, core_ref, side_ref, got_ref,
+           qh_ref, ql_ref, th_ref, tl_ref, away_ref, here_ref, core_ref, side_ref, put_ref, got_ref, raw_ref,
            load_sem, core_send, core_recv, side_send, side_recv, put_send, put_recv):
     pair, row = lax.axis_index("pair"), lax.axis_index("row")
     y_lo, core = pair // CORES, pair % CORES
@@ -203,11 +190,19 @@
     corner = (1 - y_lo) * CORES + core, 1 - y_hi
 
     slim_load = pltpu.make_async_copy(c_hbm.at[:, 0:LANES], slim_ref, load_sem.at[0])
-    x_load = pltpu.make_async_copy(x_hbm, x_ref, load_sem.at[1])
-    c_load = pltpu.make_async_copy(c_hbm, c_ref, load_sem.at[2])
+    steps = load_steps(c_hbm.shape[0])
+
+    def loads(t, start, size):
+        part = pl.ds(start, size)
+        return (
+            pltpu.make_async_copy(x_hbm.at[:, :, part], x_ref.at[:, :, part], load_sem.at[1 + 2 * t]),
+            pltpu.make_async_copy(c_hbm.at[part, :], c_ref.at[part, :], load_sem.at[2 + 2 * t]),
+        )
+
     slim_load.start()
-    x_load.start()
-    c_load.start()
+    for t, step in enumerate(steps):
+        for load in loads(t, *step):
+            load.start()
 
     barrier = pltpu.get_barrier_semaphore()
     pl.semaphore_signal(barrier, inc=1, device_id=other_core, device_id_type=MESH)
@@ -230,28 +225,38 @@
 
     slim_load.wait()
     kron, last = make_weights(pair, pair_ref, slim_ref, rows_ref)
-    x_load.wait()
-    c_load.wait()
-    sum_all_pairs(x_ref, kron, last, vh_ref, vl_ref, c_ref, ch_ref, cl_ref)
-    pl.semaphore_wait(barrier, 2 * PLANE + 1)
+
+    def sum_step(t, start, size):
+        for load in loads(t, start, size):
+            load.wait()
+        split_coeffs(c_ref, ch_ref, cl_ref, start, size)
+        sum_pairs(x_ref, kron, last, vh_ref, vl_ref, start, size)
+
+    def sum_some(t, carry):
+        sum_step(t, pl.multiple_of(t * STEP, STEP), STEP)
+        return carry
+
+    whole = sum(size == STEP for _, size in steps)
+    lax.fori_loop(0, whole, sum_some, 0)
+    for t in range(whole, len(steps)):
+        sum_step(t, *steps[t])
 
     planes = [(y_lo, 1 - y_hi), (1 - y_lo, y_hi), (1 - y_lo, 1 - y_hi), (y_lo, y_hi)]
-
-    def block(ref, k, start=0, size=ROWS):
-        return ref.at[pl.ds(k * ROWS + start, size), :]
 
     def core_copy(k):
         return pltpu.make_async_remote_copy(
-            block(away_ref, k), block(core_ref, k), core_send.at[k], core_recv.at[k],
+            away_ref.at[k], core_ref.at[k], core_send.at[k], core_recv.at[k],
             device_id=other_core, device_id_type=MESH)
 
     def spot_x(i):
         return (x + i) % X
 
+    def piece(ref, k, i):
+        return ref.at[k, :, pl.ds(pl.multiple_of(spot_x(i) * (SIDE // X), SIDE // X), SIDE // X), :]
+
     def side_copy(k, i):
-        start = spot_x(i) * PIECE
         return pltpu.make_async_remote_copy(
-            block(here_ref, k, start, PIECE), block(side_ref, k, start, PIECE), side_send.at[k, i], side_recv.at[k, i],
+            piece(here_ref, k, i), piece(side_ref, k, i), side_send.at[k, i], side_recv.at[k, i],
             device_id=other_side, device_id_type=MESH)
 
     def compute(k):
@@ -260,44 +265,45 @@
         here = (y_lo_to * CORES + core) * Y_HI + y_hi_to
         cols = [pl.ds(pl.multiple_of(side * SIDE, SIDE), SIDE) for side in (away, here)]
         c = [jnp.concatenate([ref[:, col] for col in cols], axis=1) for ref in (ch_ref, cl_ref)]
-        z = contract_s((vh_ref[...], vl_ref[...]), c)
+        for j in range(0, 8 * LANES, 256):
+            rows = slice(j, j + 256)
+            raw_ref[k // 2, rows, :] = contract_s((vh_ref[rows, :], vl_ref[rows, :]), c)
+
+    def turn(k):
         for j in range(8):
-            part = z[LANES * j : LANES * (j + 1)].T
-            away_ref[pl.ds(k * ROWS + j, SIDE, stride=8), :] = part[:SIDE]
-            here_ref[pl.ds(k * ROWS + j, SIDE, stride=8), :] = part[SIDE:]
+            part = raw_ref[k // 2, LANES * j : LANES * (j + 1), :].T
+            away_ref[k, j] = part[:SIDE]
+            here_ref[k, j] = part[SIDE:]
+        if k == 0:
+            pl.semaphore_wait(barrier, 2 * PLANE + 1)
         core_copy(k).start()
 
     def add_core(k):
         core_copy(k).wait_recv()
-        here = block(here_ref, k)
-        here[...] += block(core_ref, k)[...]
-
-    def to_side(k):
-        add_core(k)
-        for i in range(X):
-            side_copy(k, i).start()
+        here_ref[k] += core_ref[k]
 
     def put(u, t, copied_to):
         pltpu.make_async_remote_copy(
-            block(here_ref, 2 + u, t * MESSAGE, MESSAGE), got_ref.at[row], put_send.at[u], put_recv.at[u],
+            put_ref.at[u, pl.ds(t * MESSAGE, MESSAGE)], got_ref.at[row], put_send.at[u], put_recv.at[u],
             device_id=(copied_to[0], copied_to[1] * PLANE + t), device_id_type=MESH).start()
 
-    def spread(u, copied_to):
-        for i in range(X):
-            side_copy(u, i).wait_recv()
-            start = spot_x(i) * PIECE
-            here = block(here_ref, 2 + u, start, PIECE)
-            here[...] += block(side_ref, u, start, PIECE)[...]
-            own = u == 1 and i == 0
-
-            def one(t, carry):
-                put(u, spot_x(i) * Z + (spot + t) % Z, copied_to)
-                return carry
-
-            lax.fori_loop(1 if own else 0, Z, one, 0)
-            if own:
-                pltpu.make_async_copy(
-                    block(here_ref, 2 + u, spot * MESSAGE, MESSAGE), got_ref.at[row], put_recv.at[u]).start()
+    def spread(u, i):
+        copied_to = corner if u == 0 else (pair, y_hi)
+        side_copy(u, i).wait_recv()
+        both = piece(here_ref, 2 + u, i)[...] + piece(side_ref, u, i)[...]
+        start = pl.multiple_of(spot_x(i) * (ROWS // X), ROWS // X)
+        for j in range(8):
+            put_ref[u, pl.ds(start + j, SIDE // X, stride=8), :] = both[j]
+        own = u == 1 and i == 0
+
+        def one(t, carry):
+            put(u, spot_x(i) * Z + (spot + t) % Z, copied_to)
+            return carry
+
+        lax.fori_loop(1 if own else 0, Z, one, 0)
+        if own:
+            pltpu.make_async_copy(
+                put_ref.at[u, pl.ds(spot * MESSAGE, MESSAGE)], got_ref.at[row], put_recv.at[u]).start()
 
     def take(u, y_hi_from):
         got = got_ref.at[pl.ds(y_hi_from * PLANE, PLANE)]
@@ -306,17 +312,30 @@
         blocks = split(jnp.concatenate([got[:, 8 * b : 8 * b + 8, :].reshape(PLANE * 8, LANES) for b in range(local_b)], axis=1))
         return contract_r(blocks, qh_ref, ql_ref, th_ref, tl_ref, y_hi_from, PLANE, local_b)
 
+    def to_side(k):
+        add_core(k)
+        for i in range(X):
+            side_copy(k, i).start()
+
     compute(0)
+    compute(2)
+    turn(0)
+    to_side(0)
     compute(1)
-    to_side(0)
-    compute(2)
+    turn(2)
+    compute(3)
+    turn(1)
+    add_core(2)
+    spread(0, 0)
     to_side(1)
-    compute(3)
-    add_core(2)
+    spread(0, 1)
+    turn(3)
+    spread(0, 2)
     add_core(3)
-    spread(0, corner)
+    spread(0, 3)
     arrange_coeffs(c_ref, qh_ref, ql_ref, th_ref, tl_ref, Y_HI * PLANE)
-    spread(1, (pair, y_hi))
+    for i in range(X):
+        spread(1, i)
     total = take(0, 1 - y_hi)
     o_ref[...] = factor * (total + take(1, y_hi)).reshape(o_ref.shape)
 
@@ -325,8 +344,8 @@
     for k in range(2):
         for i in range(X):
             side_copy(k, i).wait_send()
-    copy_bytes_of(block(here_ref, 2), put_send.at[0])
-    copy_bytes_of(block(here_ref, 3, 0, ROWS - MESSAGE), put_send.at[1])
+    copy_bytes_of(put_ref.at[0], put_send.at[0])
+    copy_bytes_of(put_ref.at[1, pl.ds(0, ROWS - MESSAGE)], put_send.at[1])
 
 
 def body(integrals, coeffs, pair_list):
@@ -352,12 +371,14 @@
             pltpu.VMEM((3, sources * 8, orbitals), BF16),
             pltpu.VMEM((sources, orbitals), BF16),
             pltpu.VMEM((sources, orbitals), BF16),
-            pltpu.VMEM((4 * ROWS, LANES), F32),
-            pltpu.VMEM((4 * ROWS, LANES), F32),
-            pltpu.VMEM((4 * ROWS, LANES), F32),
-            pltpu.VMEM((2 * ROWS, LANES), F32),
+            pltpu.VMEM((4, 8, SIDE, LANES), F32),
+            pltpu.VMEM((4, 8, SIDE, LANES), F32),
+            pltpu.VMEM((4, 8, SIDE, LANES), F32),
+            pltpu.VMEM((2, 8, SIDE, LANES), F32),
+            pltpu.VMEM((2, ROWS, LANES), F32),
             pltpu.VMEM((sources, MESSAGE, LANES), F32),
-            pltpu.SemaphoreType.DMA((3,)),
+            pltpu.VMEM((2, 8 * LANES, 2 * SIDE), F32),
+            pltpu.SemaphoreType.DMA((1 + 2 * len(load_steps(basis)),)),
             pltpu.SemaphoreType.DMA((4,)),
             pltpu.SemaphoreType.DMA((4,)),
             pltpu.SemaphoreType.DMA((2, X)),
@@ -368,7 +389,7 @@
         compiler_params=pltpu.CompilerParams(vmem_limit_bytes=LIMIT, collective_id=0, has_side_effects=True),
         cost_estimate=pl.CostEstimate(flops=15_000_000_000, bytes_accessed=14_000_000, transcendentals=0),
         name="transform",
-    )(pair_list, integrals.transpose(1, 0, 2), coeffs)
+    )(pair_list.T, integrals.transpose(1, 0, 2), coeffs)
 
 
 def solution(mesh):

time: 78.2 us -> 61.7 us (0.79)
  Pallas kernels: 74.3 us -> 59.2 us
  local copies, waits for them, and re-layouts: 3.72 us -> 2.31 us
    pallas_call x1, Pallas kernels: 74.3 us -> 59.2 us  [body(): pl.pallas_call(functools.partial(kernel, factor), out_shape=jax.ShapeDtyp...]
    unnamed x2 -> x1, local copies, waits for them, and re-layouts: 3.72 us -> 2.31 us
where the time goes in v3:
time: 61.7 us; the launch traced here: 61.5 us
  Pallas kernels  59.2 us (96%)
  local copies, waits for them, and re-layouts  2.31 us (4%)
    pallas_call x1, Pallas kernels, body(): pl.pallas_call(functools.partial(kernel, factor), out_shape=jax.ShapeDtyp...  59.2 us
    unnamed x1, local copies, waits for them, and re-layouts  2.31 us

profile of v3, /device:TPU:1, one launch (start us, length us, event | category | flops | bytes accessed | tf_op | source)
XLA Modules:
  0.0 61.5 jit_solution(17379535761321242968)
XLA Ops:
  0.0 59.2 %transform.1 = f32[4,64,1024]{2,1,0:T(8,128)} custom-call(s32[2,128]{1,0:T(2,128)} %bitcast.3, f32[25,32,1600]{2,1,0:T(8,128)} %bitcast.2, f32[1600,1024]{1,0:T(8,128)} %c_hbm.1), custom_call_target="tpu_custom_call" | custom-call | flops 15000000512 | bytes 14000000 | tf_op jit(solution)/shard_map/transform/pallas_call | solution.py:356
  59.2 2.3 %copy.5 = f32[4,64,1024]{2,1,0:T(8,128)} copy(f32[4,64,1024]{2,1,0:T(8,128)} %transform.1) | data formatting | bytes 2097152

commit v4 on v3

--- a/solution.py
+++ b/solution.py
@@ -179,7 +179,7 @@
 
 
 def kernel(factor, pair_ref, x_hbm, c_hbm, o_ref, x_ref, c_ref, slim_ref, rows_ref, vh_ref, vl_ref, ch_ref, cl_ref,
-           qh_ref, ql_ref, th_ref, tl_ref, away_ref, here_ref, core_ref, side_ref, put_ref, got_ref, raw_ref,
+           qh_ref, ql_ref, th_ref, tl_ref, away_ref, here_ref, core_ref, side_ref, put_ref, got_ref,
            load_sem, core_send, core_recv, side_send, side_recv, put_send, put_recv):
     pair, row = lax.axis_index("pair"), lax.axis_index("row")
     y_lo, core = pair // CORES, pair % CORES
@@ -265,15 +265,17 @@
         here = (y_lo_to * CORES + core) * Y_HI + y_hi_to
         cols = [pl.ds(pl.multiple_of(side * SIDE, SIDE), SIDE) for side in (away, here)]
         c = [jnp.concatenate([ref[:, col] for col in cols], axis=1) for ref in (ch_ref, cl_ref)]
-        for j in range(0, 8 * LANES, 256):
-            rows = slice(j, j + 256)
-            raw_ref[k // 2, rows, :] = contract_s((vh_ref[rows, :], vl_ref[rows, :]), c)
-
-    def turn(k):
-        for j in range(8):
-            part = raw_ref[k // 2, LANES * j : LANES * (j + 1), :].T
-            away_ref[k, j] = part[:SIDE]
-            here_ref[k, j] = part[SIDE:]
+        ready = None
+        for start in range(0, 8 * LANES + 256, 256):
+            done = ready
+            if start < 8 * LANES:
+                rows = slice(start, start + 256)
+                ready = start, contract_s((vh_ref[rows, :], vl_ref[rows, :]), c)
+            if done is not None:
+                for part in range(0, 256, LANES):
+                    turned = done[1][part : part + LANES].T
+                    away_ref[k, (done[0] + part) // LANES] = turned[:SIDE]
+                    here_ref[k, (done[0] + part) // LANES] = turned[SIDE:]
         if k == 0:
             pl.semaphore_wait(barrier, 2 * PLANE + 1)
         core_copy(k).start()
@@ -318,18 +320,14 @@
             side_copy(k, i).start()
 
     compute(0)
+    to_side(0)
     compute(2)
-    turn(0)
-    to_side(0)
     compute(1)
-    turn(2)
-    compute(3)
-    turn(1)
     add_core(2)
     spread(0, 0)
     to_side(1)
     spread(0, 1)
-    turn(3)
+    compute(3)
     spread(0, 2)
     add_core(3)
     spread(0, 3)
@@ -377,7 +375,6 @@
             pltpu.VMEM((2, 8, SIDE, LANES), F32),
             pltpu.VMEM((2, ROWS, LANES), F32),
             pltpu.VMEM((sources, MESSAGE, LANES), F32),
-            pltpu.VMEM((2, 8 * LANES, 2 * SIDE), F32),
             pltpu.SemaphoreType.DMA((1 + 2 * len(load_steps(basis)),)),
             pltpu.SemaphoreType.DMA((4,)),
             pltpu.SemaphoreType.DMA((4,)),

time: 61.7 us -> 59.2 us (0.959)
  Pallas kernels: 59.2 us -> 56.7 us
    pallas_call x1, Pallas kernels: 59.2 us -> 56.7 us  [body(): pl.pallas_call(functools.partial(kernel, factor), out_shape=jax.ShapeDtyp...]
where the time goes in v4:
time: 59.2 us; the launch traced here: 59 us
  Pallas kernels  56.7 us (96%)
  local copies, waits for them, and re-layouts  2.31 us (4%)
    pallas_call x1, Pallas kernels, body(): pl.pallas_call(functools.partial(kernel, factor), out_shape=jax.ShapeDtyp...  56.7 us
    unnamed x1, local copies, waits for them, and re-layouts  2.31 us

profile of v4, /device:TPU:1, one launch (start us, length us, event | category | flops | bytes accessed | tf_op | source)
XLA Modules:
  0.0 59.0 jit_solution(18113665963035972251)
XLA Ops:
  0.0 56.7 %transform.1 = f32[4,64,1024]{2,1,0:T(8,128)} custom-call(s32[2,128]{1,0:T(2,128)} %bitcast.3, f32[25,32,1600]{2,1,0:T(8,128)} %bitcast.2, f32[1600,1024]{1,0:T(8,128)} %c_hbm.1), custom_call_target="tpu_custom_call" | custom-call | flops 15000000512 | bytes 14000000 | tf_op jit(solution)/shard_map/transform/pallas_call | solution.py:354
  56.7 2.3 %copy.5 = f32[4,64,1024]{2,1,0:T(8,128)} copy(f32[4,64,1024]{2,1,0:T(8,128)} %transform.1) | data formatting | bytes 2097152

commit v5 on v4

--- a/solution.py
+++ b/solution.py
@@ -189,6 +189,25 @@
     other_side = ((1 - y_lo) * CORES + core, row)
     corner = (1 - y_lo) * CORES + core, 1 - y_hi
 
+    barrier = pltpu.get_barrier_semaphore()
+    pl.semaphore_signal(barrier, inc=1, device_id=other_core, device_id_type=MESH)
+    pl.semaphore_signal(barrier, inc=1, device_id=other_side, device_id_type=MESH)
+
+    def greet(t, carry):
+        pl.semaphore_signal(
+            barrier, inc=1, device_id=(corner[0], corner[1] * PLANE + t), device_id_type=MESH
+        )
+        return carry
+
+    def greet_own(t, carry):
+        pl.semaphore_signal(
+            barrier, inc=1, device_id=(pair, y_hi * PLANE + (spot + t) % PLANE), device_id_type=MESH
+        )
+        return carry
+
+    lax.fori_loop(0, PLANE, greet, 0)
+    lax.fori_loop(1, PLANE, greet_own, 0)
+
     slim_load = pltpu.make_async_copy(c_hbm.at[:, 0:LANES], slim_ref, load_sem.at[0])
     steps = load_steps(c_hbm.shape[0])
 
@@ -203,25 +222,6 @@
     for t, step in enumerate(steps):
         for load in loads(t, *step):
             load.start()
-
-    barrier = pltpu.get_barrier_semaphore()
-    pl.semaphore_signal(barrier, inc=1, device_id=other_core, device_id_type=MESH)
-    pl.semaphore_signal(barrier, inc=1, device_id=other_side, device_id_type=MESH)
-
-    def greet(t, carry):
-        pl.semaphore_signal(
-            barrier, inc=1, device_id=(corner[0], corner[1] * PLANE + t), device_id_type=MESH
-        )
-        return carry
-
-    def greet_own(t, carry):
-        pl.semaphore_signal(
-            barrier, inc=1, device_id=(pair, y_hi * PLANE + (spot + t) % PLANE), device_id_type=MESH
-        )
-        return carry
-
-    lax.fori_loop(0, PLANE, greet, 0)
-    lax.fori_loop(1, PLANE, greet_own, 0)
 
     slim_load.wait()
     kron, last = make_weights(pair, pair_ref, slim_ref, rows_ref)
@@ -331,8 +331,9 @@
     spread(0, 2)
     add_core(3)
     spread(0, 3)
+    spread(1, 0)
     arrange_coeffs(c_ref, qh_ref, ql_ref, th_ref, tl_ref, Y_HI * PLANE)
-    for i in range(X):
+    for i in range(1, X):
         spread(1, i)
     total = take(0, 1 - y_hi)
     o_ref[...] = factor * (total + take(1, y_hi)).reshape(o_ref.shape)

time: 59.2 us -> 60.2 us (1.017)
  Pallas kernels: 56.7 us -> 57.8 us
    pallas_call x1, Pallas kernels: 56.7 us -> 57.8 us  [body(): pl.pallas_call(functools.partial(kernel, factor), out_shape=jax.ShapeDtyp...]
where the time goes in v5:
time: 60.2 us; the launch traced here: 60.1 us
  Pallas kernels  57.8 us (96%)
  local copies, waits for them, and re-layouts  2.31 us (4%)
    pallas_call x1, Pallas kernels, body(): pl.pallas_call(functools.partial(kernel, factor), out_shape=jax.ShapeDtyp...  57.8 us
    unnamed x1, local copies, waits for them, and re-layouts  2.31 us

profile of v5, /device:TPU:1, one launch (start us, length us, event | category | flops | bytes accessed | tf_op | source)
XLA Modules:
  0.0 60.1 jit_solution(18161121415816127635)
XLA Ops:
  0.0 57.8 %transform.1 = f32[4,64,1024]{2,1,0:T(8,128)} custom-call(s32[2,128]{1,0:T(2,128)} %bitcast.3, f32[25,32,1600]{2,1,0:T(8,128)} %bitcast.2, f32[1600,1024]{1,0:T(8,128)} %c_hbm.1), custom_call_target="tpu_custom_call" | custom-call | flops 15000000512 | bytes 14000000 | tf_op jit(solution)/shard_map/transform/pallas_call | solution.py:355
  57.8 2.3 %copy.5 = f32[4,64,1024]{2,1,0:T(8,128)} copy(f32[4,64,1024]{2,1,0:T(8,128)} %transform.1) | data formatting | bytes 2097152
